TPU v7x, 32 devices: a whole 2x2x4 slice. The times are simulated.
32 devices in a mesh: seq: 16 (over z, x, core), section: 2 (over y).
Axes of the slice: x: 2, y: 2, z: 4, core: 2. Of those that a mesh axis runs over, the one named last changes fastest.
Arguments:
- fwd_input: bfloat16 [2, 4096, 768], P('section', 'seq'), may hold values from -6 to 6
- bwd_input: bfloat16 [2, 4096, 768], P('section', 'seq'), may hold values from -6 to 6
- bwd_cotangent: bfloat16 [2, 4096, 768], P('section', 'seq'), may hold values from -6 to 6
- conv_weight: bfloat16 [2, 2, 3, 768, 384], P('section', None, None, 'seq'), may hold values from -0.125 to 0.125
- proj_weight: bfloat16 [2, 2, 384, 768], P('section', None, 'seq'), may hold values from -0.3125 to 0.3125
Outputs:
- next_input: bfloat16 [2, 4096, 768], P('section', 'seq')
- prev_cotangent: bfloat16 [2, 4096, 768], P('section', 'seq')
All inputs are finite; a program needn't handle non-finite values.
Results may differ from a plain program's by a relative error of at most 0.012.
Values may be sent and summed in bfloat16 or wider, within the bound.
A program may use at most 64 MiB of HBM per device.

v0:
```python
import jax
import jax.numpy as jnp
from jax import lax
from jax.sharding import PartitionSpec as P

BLOCKS = 2
FIRST_DILATION = 128


def padded(x, sides, width):
    for axis, dim in sides:
        size, length = (lax.axis_size(axis), x.shape[dim])
        up = [(i, (i + 1) % size) for i in range(size - 1)]
        down = [(j, i) for i, j in up]
        last = lax.slice_in_dim(x, length - width, length, axis=dim)
        initial = lax.slice_in_dim(x, 0, width, axis=dim)
        before = lax.ppermute(last, axis, up)
        after = lax.ppermute(initial, axis, down)
        x = jnp.concatenate([before, x, after], axis=dim)
    return x


def from_behind(block, axis, distance):
    devices = range(lax.axis_size(axis))
    route = [(i - distance, i) for i in devices if i - distance in devices]
    return lax.ppermute(block, axis, route)


def from_behind_2(block, axis, distance):
    devices = range(lax.axis_size(axis))
    route = [((i - distance) % len(devices), i) for i in devices]
    return lax.ppermute(block, axis, route)


def gelu_back(value, cotangent):
    return jax.vjp(jax.nn.gelu, value)[1](cotangent)[0]


def rounded(product):
    return lax.optimization_barrier(product.astype(jnp.bfloat16)).astype(jnp.float32)


def reach(values, spacing_gap):
    length = values.shape[1]
    if spacing_gap < length:
        padded_input = padded(values, (("seq", 1),), spacing_gap)
        return (padded_input[:, :length], padded_input[:, 2 * spacing_gap :])
    shard_hops = spacing_gap // length
    earlier = from_behind(values, "seq", shard_hops)
    later = from_behind(values, "seq", -shard_hops)
    return (earlier, later)


def conv_apply(values, weight):
    return jnp.einsum("krc,ch->krh", values, weight, preferred_element_type=jnp.float32)


def conv_transpose(values, weight):
    return jnp.einsum("krh,ch->krc", values, weight, preferred_element_type=jnp.float32)


def run_forward(present_state, pieces):
    stored = []
    for depth_level in range(BLOCKS):
        conv_part, proj_part = pieces[depth_level]
        spacing_gap = FIRST_DILATION * 4**depth_level
        activated = jax.nn.gelu(present_state.astype(jnp.float32)).astype(jnp.bfloat16)
        middle = conv_apply(activated, conv_part[1])
        earlier, later = reach(activated, spacing_gap)
        preact = (
            rounded(conv_apply(earlier, conv_part[0]))
            + middle
            + rounded(conv_apply(later, conv_part[2]))
        )
        hidden = jax.nn.gelu(preact).astype(jnp.bfloat16)
        stored.append((present_state, preact))
        branch = jnp.einsum("krh,hc->krc", hidden, proj_part, preferred_element_type=jnp.float32)
        present_state = (present_state.astype(jnp.float32) + branch).astype(jnp.bfloat16)
    return (present_state, stored)


def local(fwd_input, bwd_input, bwd_cotangent, conv_weight, proj_weight):
    convolution_complete, proj_full = (
        lax.all_gather(conv_weight, "seq", axis=3, tiled=True),
        lax.all_gather(proj_weight, "seq", axis=2, tiled=True),
    )
    pieces = [
        (convolution_complete[0, depth_level], proj_full[0, depth_level])
        for depth_level in range(BLOCKS)
    ]
    forward_out, unused = run_forward(fwd_input, pieces)
    unused_out, stored = run_forward(bwd_input, pieces)
    cotangent = bwd_cotangent
    for depth_level in reversed(range(BLOCKS)):
        conv_part, proj_part = pieces[depth_level]
        spacing_gap = FIRST_DILATION * 4**depth_level
        block_in, preact = stored[depth_level]
        d_hidden = jnp.einsum(
            "krc,hc->krh", cotangent, proj_part, preferred_element_type=jnp.float32
        )
        d_preact = gelu_back(preact, d_hidden).astype(jnp.bfloat16)
        earlier, later = reach(d_preact, spacing_gap)
        d_act = (
            conv_transpose(later, conv_part[0])
            + conv_transpose(d_preact, conv_part[1])
            + conv_transpose(earlier, conv_part[2])
        )
        total = cotangent.astype(jnp.float32) + gelu_back(block_in.astype(jnp.float32), d_act)
        cotangent = total.astype(jnp.bfloat16)
    next_input = from_behind_2(forward_out, "section", 1)
    prev_cotangent = from_behind_2(cotangent, "section", -1)
    return (next_input, prev_cotangent)


def solution(mesh):
    in_specs = (
        P("section", "seq", None),
        P("section", "seq", None),
        P("section", "seq", None),
        P("section", None, None, "seq", None),
        P("section", None, "seq", None),
    )
    out_specs = (P("section", "seq", None), P("section", "seq", None))
    return jax.shard_map(local, mesh=mesh, in_specs=in_specs, out_specs=out_specs, check_vma=False)
```

profile of v0, /device:TPU:8, one launch (start us, length us, event | category | flops | bytes accessed | tf_op | source)
XLA Modules:
  0.0 184.0 jit_solution(14636914586772354015)
XLA Ops:
  10.0 1.9 %collective-permute-start.5 = (bf16[1,128,768]{2,1,0:T(8,128)(2,1)S(1)}, bf16[1,128,768]{2,1,0:T(8,128)(2,1)S(1)}, u32[]{:S(2)}, u32[]{:S(2)}) collective-permute-start(bf16[1,128,768]{2,1,0:T(8,128)(2,1)S(1)} %get-tuple-element.2), channel_id=1, source_target_pairs={{0,2},{2,4},{4,6},{6,8},{8,10},{10,12},{12,14},{14,16},{16,18},{18... | collective-permute-start | bytes 589832 | tf_op jit(solution)/shard_map/ppermute | solution.py:17
  11.9 4.5 %collective-permute-start.6 = (bf16[1,128,768]{2,1,0:T(8,128)(2,1)S(1)}, bf16[1,128,768]{2,1,0:T(8,128)(2,1)S(1)}, u32[]{:S(2)}, u32[]{:S(2)}) collective-permute-start(bf16[1,128,768]{2,1,0:T(8,128)(2,1)S(1)} %get-tuple-element.3), channel_id=1, source_target_pairs={{2,0},{4,2},{6,4},{8,6},{10,8},{12,10},{14,12},{16,14},{18,16},{20... | collective-permute-start | bytes 589832 | tf_op jit(solution)/shard_map/ppermute | solution.py:18
  19.2 1.9 %collective-permute-start = (bf16[1,128,768]{2,1,0:T(8,128)(2,1)}, bf16[1,128,768]{2,1,0:T(8,128)(2,1)}, u32[]{:S(2)}, u32[]{:S(2)}) collective-permute-start(bf16[1,128,768]{2,1,0:T(8,128)(2,1)} %get-tuple-element.4), channel_id=1, source_target_pairs={{0,2},{2,4},{4,6},{6,8},{8,10},{10,12},{12,14},{14,16},{16,18},{18... | collective-permute-start | bytes 589832 | tf_op jit(solution)/shard_map/ppermute | solution.py:17
  21.2 4.5 %collective-permute-start.1 = (bf16[1,128,768]{2,1,0:T(8,128)(2,1)}, bf16[1,128,768]{2,1,0:T(8,128)(2,1)}, u32[]{:S(2)}, u32[]{:S(2)}) collective-permute-start(bf16[1,128,768]{2,1,0:T(8,128)(2,1)} %get-tuple-element.5), channel_id=1, source_target_pairs={{2,0},{4,2},{6,4},{8,6},{10,8},{12,10},{14,12},{16,14},{18,16},{20... | collective-permute-start | bytes 589832 | tf_op jit(solution)/shard_map/ppermute | solution.py:18
  25.7 34.0 %all-gather.3.cloned.1.call-done = bf16[1,2,3,768,384]{4,3,2,1,0:T(8,128)(2,1)} async-done(((bf16[1,2,3,48,384]{4,3,2,1,0:T(8,128)(2,1)}), bf16[1,2,3,768,384]{4,3,2,1,0:T(8,128)(2,1)}) %all-gather.3.cloned.1.call-update) | async-done | bytes 3538960 | tf_op jit(solution)/shard_map/all_gather | solution.py:84
  59.7 1.4 fusion.19
  61.2 1.4 fusion.20
  62.6 2.5 %fusion.12 = f32[1,256,384]{2,1,0:T(8,128)} fusion(bf16[1,2,3,768,384]{4,3,2,1,0:T(8,128)(2,1)} %all-gather.3.cloned.1.call-done, bf16[1,256,384]{2,1,0:T(8,128)(2,1)S(1)} %fusion.20, bf16[1,256,384]{2,1,0:T(8,128)(2,1)S(1)} %fusion.19, bf16[1,256,768]{2,1,0:T(8,128)(2,1)} %param.6), kind=kOutput, calls=%fused_computation.44 | convolution fusion | flops 153354240 | bytes 1769472 | tf_op jit(solution)/shard_map/krc,ch->krh/dot_general | solution.py:55
  65.2 32.6 %all-gather.5.cloned.1.call-done = bf16[1,2,384,768]{3,2,1,0:T(8,128)(2,1)} async-done(((bf16[1,2,24,768]{3,2,1,0:T(8,128)(2,1)}), bf16[1,2,384,768]{3,2,1,0:T(8,128)(2,1)}) %all-gather.5.cloned.1.call-update) | async-done | bytes 1179664 | tf_op jit(solution)/shard_map/all_gather | solution.py:85
  97.8 2.8 %fusion.48 = (bf16[1,256,768]{2,1,0:T(8,128)(2,1)}, bf16[1,256,768]{2,1,0:T(8,128)(2,1)}) fusion(bf16[1,2,384,768]{3,2,1,0:T(8,128)(2,1)} %all-gather.5.cloned.1.call-done, f32[1,256,384]{2,1,0:T(8,128)} %fusion.12, bf16[1,256,768]{2,1,0:T(8,128)(2,1)} %param.6), kind=kOutput, calls=%fused_computation.88 | convolution fusion | flops 154435584 | bytes 2162688 | tf_op jit(solution)/shard_map/krh,hc->krc/dot_general | solution.py:77
  100.5 3.0 %collective-permute-start.7 = (bf16[1,256,768]{2,1,0:T(8,128)(2,1)}, bf16[1,256,768]{2,1,0:T(8,128)(2,1)}, u32[]{:S(2)}, u32[]{:S(2)}) collective-permute-start(bf16[1,256,768]{2,1,0:T(8,128)(2,1)} %get-tuple-element.10), channel_id=1, source_target_pairs={{0,4},{2,6},{4,8},{6,10},{8,12},{10,14},{12,16},{14,18},{16,20},{1... | collective-permute-start | bytes 1179656 | tf_op jit(solution)/shard_map/ppermute | solution.py:26
  103.5 3.8 %collective-permute-start.8 = (bf16[1,256,768]{2,1,0:T(8,128)(2,1)}, bf16[1,256,768]{2,1,0:T(8,128)(2,1)}, u32[]{:S(2)}, u32[]{:S(2)}) collective-permute-start(bf16[1,256,768]{2,1,0:T(8,128)(2,1)} %get-tuple-element.10), channel_id=1, source_target_pairs={{4,0},{6,2},{8,4},{10,6},{12,8},{14,10},{16,12},{18,14},{20,16},{2... | collective-permute-start | bytes 1179656 | tf_op jit(solution)/shard_map/ppermute | solution.py:26
  107.3 2.0 %fusion.15 = bf16[1,256,384]{2,1,0:T(8,128)(2,1)} fusion(bf16[1,2,3,768,384]{4,3,2,1,0:T(8,128)(2,1)S(1)} %copy-done, bf16[1,256,768]{2,1,0:T(8,128)(2,1)S(1)} %copy-done.2, bf16[1,128,768]{2,1,0:T(8,128)(2,1)} %collective-permute-done), kind=kOutput, calls=%fused_computation.55 | convolution fusion | flops 151879680 | bytes 1376256 | tf_op jit(solution)/shard_map/krc,ch->krh/dot_general | solution.py:55
  109.3 2.0 %fusion.16 = bf16[1,256,384]{2,1,0:T(8,128)(2,1)} fusion(bf16[1,2,3,768,384]{4,3,2,1,0:T(8,128)(2,1)S(1)} %copy-done, bf16[1,128,768]{2,1,0:T(8,128)(2,1)} %collective-permute-done.1, bf16[1,256,768]{2,1,0:T(8,128)(2,1)S(1)} %copy-done.2), kind=kOutput, calls=%fused_computation.56 | convolution fusion | flops 151879680 | bytes 1376256 | tf_op jit(solution)/shard_map/krc,ch->krh/dot_general | solution.py:55
  111.3 3.3 %fusion.44 = (bf16[1,256,768]{2,1,0:T(8,128)(2,1)}, bf16[1,256,768]{2,1,0:T(8,128)(2,1)}) fusion(bf16[1,2,384,768]{3,2,1,0:T(8,128)(2,1)} %all-gather.5.cloned.1.call-done, bf16[1,2,3,768,384]{4,3,2,1,0:T(8,128)(2,1)S(1)} %copy-done, bf16[1,256,384]{2,1,0:T(8,128)(2,1)} %fusion.16, bf16[1,256,384]{2,1,0:T(8,128)(2,1)} %fusion.15, bf16[1,256,768]{2,1,0:T(8,128)(2,1)} %param.5), kind=kOutput, calls=%fused_computation.84 | convolution fusion | flops 307789824 | bytes 3145728 | tf_op jit(solution)/shard_map/krh,hc->krc/dot_general | solution.py:77
  114.5 2.2 %collective-permute-start.2 = (bf16[1,256,768]{2,1,0:T(8,128)(2,1)}, bf16[1,256,768]{2,1,0:T(8,128)(2,1)S(1)}, u32[]{:S(2)}, u32[]{:S(2)}) collective-permute-start(bf16[1,256,768]{2,1,0:T(8,128)(2,1)} %get-tuple-element.8), channel_id=1, source_target_pairs={{0,4},{2,6},{4,8},{6,10},{8,12},{10,14},{12,16},{14,18},{16,20},{1... | collective-permute-start | bytes 1179656 | tf_op jit(solution)/shard_map/ppermute | solution.py:26
  116.8 4.6 %collective-permute-start.3 = (bf16[1,256,768]{2,1,0:T(8,128)(2,1)}, bf16[1,256,768]{2,1,0:T(8,128)(2,1)S(1)}, u32[]{:S(2)}, u32[]{:S(2)}) collective-permute-start(bf16[1,256,768]{2,1,0:T(8,128)(2,1)} %get-tuple-element.8), channel_id=1, source_target_pairs={{4,0},{6,2},{8,4},{10,6},{12,8},{14,10},{16,12},{18,14},{20,16},{2... | collective-permute-start | bytes 1179656 | tf_op jit(solution)/shard_map/ppermute | solution.py:26
  121.8 1.4 fusion.21
  123.1 8.7 %collective-permute-done.8 = bf16[1,256,768]{2,1,0:T(8,128)(2,1)} collective-permute-done((bf16[1,256,768]{2,1,0:T(8,128)(2,1)}, bf16[1,256,768]{2,1,0:T(8,128)(2,1)}, u32[]{:S(2)}, u32[]{:S(2)}) %collective-permute-start.8) | collective-permute-done | bytes 393248 | tf_op jit(solution)/shard_map/ppermute | solution.py:26
  131.8 1.4 fusion.22
  133.2 1.4 fusion.14
  135.8 4.0 %collective-permute-start.10 = (bf16[1,256,384]{2,1,0:T(8,128)(2,1)}, bf16[1,256,384]{2,1,0:T(8,128)(2,1)}, u32[]{:S(2)}, u32[]{:S(2)}) collective-permute-start(bf16[1,256,384]{2,1,0:T(8,128)(2,1)} %fusion.74), channel_id=1, source_target_pairs={{0,4},{2,6},{4,8},{6,10},{8,12},{10,14},{12,16},{14,18},{16,20},{1... | collective-permute-start | bytes 589832 | tf_op jit(solution)/shard_map/ppermute | solution.py:26
  139.9 2.7 %collective-permute-start.9 = (bf16[1,256,384]{2,1,0:T(8,128)(2,1)}, bf16[1,256,384]{2,1,0:T(8,128)(2,1)}, u32[]{:S(2)}, u32[]{:S(2)}) collective-permute-start(bf16[1,256,384]{2,1,0:T(8,128)(2,1)} %fusion.74), channel_id=1, source_target_pairs={{4,0},{6,2},{8,4},{10,6},{12,8},{14,10},{16,12},{18,14},{20,16},{2... | collective-permute-start | bytes 589832 | tf_op jit(solution)/shard_map/ppermute | solution.py:26
  144.7 3.0 %fusion.5 = bf16[1,256,768]{2,1,0:T(8,128)(2,1)} fusion(bf16[1,256,768]{2,1,0:T(8,128)(2,1)} %get-tuple-element.9, bf16[1,2,384,768]{3,2,1,0:T(8,128)(2,1)} %all-gather.5.cloned.1.call-done, bf16[1,2,3,768,384]{4,3,2,1,0:T(8,128)(2,1)S(1)} %copy-done, bf16[1,256,384]{2,1,0:T(8,128)(2,1)} %fusion.18, bf16[1,256,384]{2,1,0:T(8,128)(2,1)} %fusion.17), kind=kOutput, calls=%fused_computation.31 | convolution fusion | flops 305823744 | bytes 2752512 | tf_op jit(solution)/shard_map/krh,hc->krc/dot_general | solution.py:77
  147.7 1.5 collective-permute-start.4
  149.2 1.3 fusion.59
  150.5 1.4 fusion.60
  152.0 2.0 %fusion.32 = bf16[1,256,768]{2,1,0:T(8,128)(2,1)S(1)} fusion(bf16[1,256,768]{2,1,0:T(8,128)(2,1)} %get-tuple-element.11, f32[256,768]{1,0:T(8,128)S(1)} %fusion.60, f32[256,768]{1,0:T(8,128)S(1)} %fusion.59, bf16[1,256,768]{2,1,0:T(8,128)(2,1)} %param.7, bf16[1,2,3,768,384]{4,3,2,1,0:T(8,128)(2,1)S(1)} %copy-done, ...), kind=kOutput, calls=%fused_computation.72 | convolution fusion | flops 155910144 | bytes 3538944 | tf_op jit(solution)/shard_map/krh,ch->krc/dot_general | solution.py:59
  154.5 1.9 %collective-permute-start.12 = (bf16[1,128,384]{2,1,0:T(8,128)(2,1)S(1)}, bf16[1,128,384]{2,1,0:T(8,128)(2,1)S(1)}, u32[]{:S(2)}, u32[]{:S(2)}) collective-permute-start(bf16[1,128,384]{2,1,0:T(8,128)(2,1)S(1)} %get-tuple-element.7), channel_id=1, source_target_pairs={{0,2},{2,4},{4,6},{6,8},{8,10},{10,12},{12,14},{14,16},{16,18},{18... | collective-permute-start | bytes 294920 | tf_op jit(solution)/shard_map/ppermute | solution.py:17
  156.5 4.5 %collective-permute-start.11 = (bf16[1,128,384]{2,1,0:T(8,128)(2,1)S(1)}, bf16[1,128,384]{2,1,0:T(8,128)(2,1)S(1)}, u32[]{:S(2)}, u32[]{:S(2)}) collective-permute-start(bf16[1,128,384]{2,1,0:T(8,128)(2,1)S(1)} %get-tuple-element.6), channel_id=1, source_target_pairs={{2,0},{4,2},{6,4},{8,6},{10,8},{12,10},{14,12},{16,14},{18,16},{20... | collective-permute-start | bytes 294920 | tf_op jit(solution)/shard_map/ppermute | solution.py:18
  161.8 1.4 collective-permute-done.11
  164.6 11.0 %collective-permute-done.13 = bf16[1,256,768]{2,1,0:T(8,128)(2,1)S(1)} collective-permute-done((bf16[1,256,768]{2,1,0:T(8,128)(2,1)S(1)}, bf16[1,256,768]{2,1,0:T(8,128)(2,1)S(1)}, u32[]{:S(2)}, u32[]{:S(2)}) %collective-permute-start.13) | collective-permute-done | bytes 393248 | tf_op jit(solution)/shard_map/ppermute | solution.py:32
  (46 shorter events, 13.4 us)
Async XLA Ops:
  7.2 52.6 %all-gather.3.cloned.1.call-start = ((), (), s32[]{:S(2)}) async-start(), calls=%async_computation | async-start | bytes 3760128 | tf_op jit(solution)/shard_map/all_gather | solution.py:84
  7.9 89.9 %all-gather.5.cloned.1.call-start = ((), (), s32[]{:S(2)}) async-start(), calls=%async_computation.1 | async-start | bytes 1253376 | tf_op jit(solution)/shard_map/all_gather | solution.py:85
  10.0 15.8 %collective-permute-start.5 = (bf16[1,128,768]{2,1,0:T(8,128)(2,1)S(1)}, bf16[1,128,768]{2,1,0:T(8,128)(2,1)S(1)}, u32[]{:S(2)}, u32[]{:S(2)}) collective-permute-start(bf16[1,128,768]{2,1,0:T(8,128)(2,1)S(1)} %get-tuple-element.2), channel_id=1, source_target_pairs={{0,2},{2,4},{4,6},{6,8},{8,10},{10,12},{12,14},{14,16},{16,18},{18... | collective-permute-start | bytes 589832 | tf_op jit(solution)/shard_map/ppermute | solution.py:17
  11.9 49.3 %collective-permute-start.6 = (bf16[1,128,768]{2,1,0:T(8,128)(2,1)S(1)}, bf16[1,128,768]{2,1,0:T(8,128)(2,1)S(1)}, u32[]{:S(2)}, u32[]{:S(2)}) collective-permute-start(bf16[1,128,768]{2,1,0:T(8,128)(2,1)S(1)} %get-tuple-element.3), channel_id=1, source_target_pairs={{2,0},{4,2},{6,4},{8,6},{10,8},{12,10},{14,12},{16,14},{18,16},{20... | collective-permute-start | bytes 589832 | tf_op jit(solution)/shard_map/ppermute | solution.py:18
  17.7 0.7 copy-start.1
  19.2 88.0 %collective-permute-start = (bf16[1,128,768]{2,1,0:T(8,128)(2,1)}, bf16[1,128,768]{2,1,0:T(8,128)(2,1)}, u32[]{:S(2)}, u32[]{:S(2)}) collective-permute-start(bf16[1,128,768]{2,1,0:T(8,128)(2,1)} %get-tuple-element.4), channel_id=1, source_target_pairs={{0,2},{2,4},{4,6},{6,8},{8,10},{10,12},{12,14},{14,16},{16,18},{18... | collective-permute-start | bytes 589832 | tf_op jit(solution)/shard_map/ppermute | solution.py:17
  21.2 88.1 %collective-permute-start.1 = (bf16[1,128,768]{2,1,0:T(8,128)(2,1)}, bf16[1,128,768]{2,1,0:T(8,128)(2,1)}, u32[]{:S(2)}, u32[]{:S(2)}) collective-permute-start(bf16[1,128,768]{2,1,0:T(8,128)(2,1)} %get-tuple-element.5), channel_id=1, source_target_pairs={{2,0},{4,2},{6,4},{8,6},{10,8},{12,10},{14,12},{16,14},{18,16},{20... | collective-permute-start | bytes 589832 | tf_op jit(solution)/shard_map/ppermute | solution.py:18
  62.6 44.7 %copy-start = (bf16[1,2,3,768,384]{4,3,2,1,0:T(8,128)(2,1)S(1)}, bf16[1,2,3,768,384]{4,3,2,1,0:T(8,128)(2,1)}, u32[]{:S(2)}) copy-start(bf16[1,2,3,768,384]{4,3,2,1,0:T(8,128)(2,1)} %all-gather.3.cloned.1.call-done) | copy-start | bytes 10616836
  97.8 9.5 %copy-start.2 = (bf16[1,256,768]{2,1,0:T(8,128)(2,1)S(1)}, bf16[1,256,768]{2,1,0:T(8,128)(2,1)}, u32[]{:S(2)}) copy-start(bf16[1,256,768]{2,1,0:T(8,128)(2,1)} %copy-done.1) | copy-start | bytes 1179652
  100.5 21.3 %collective-permute-start.7 = (bf16[1,256,768]{2,1,0:T(8,128)(2,1)}, bf16[1,256,768]{2,1,0:T(8,128)(2,1)}, u32[]{:S(2)}, u32[]{:S(2)}) collective-permute-start(bf16[1,256,768]{2,1,0:T(8,128)(2,1)} %get-tuple-element.10), channel_id=1, source_target_pairs={{0,4},{2,6},{4,8},{6,10},{8,12},{10,14},{12,16},{14,18},{16,20},{1... | collective-permute-start | bytes 1179656 | tf_op jit(solution)/shard_map/ppermute | solution.py:26
  103.5 28.3 %collective-permute-start.8 = (bf16[1,256,768]{2,1,0:T(8,128)(2,1)}, bf16[1,256,768]{2,1,0:T(8,128)(2,1)}, u32[]{:S(2)}, u32[]{:S(2)}) collective-permute-start(bf16[1,256,768]{2,1,0:T(8,128)(2,1)} %get-tuple-element.10), channel_id=1, source_target_pairs={{4,0},{6,2},{8,4},{10,6},{12,8},{14,10},{16,12},{18,14},{20,16},{2... | collective-permute-start | bytes 1179656 | tf_op jit(solution)/shard_map/ppermute | solution.py:26
  114.5 20.1 %copy-start.4 = (bf16[1,2,384,768]{3,2,1,0:T(8,128)(2,1)S(1)}, bf16[1,2,384,768]{3,2,1,0:T(8,128)(2,1)}, u32[]{:S(2)}) copy-start(bf16[1,2,384,768]{3,2,1,0:T(8,128)(2,1)} %all-gather.5.cloned.1.call-done) | copy-start | bytes 3538948
  114.5 20.1 %copy-start.6 = (bf16[1,256,768]{2,1,0:T(8,128)(2,1)S(1)}, bf16[1,256,768]{2,1,0:T(8,128)(2,1)}, u32[]{:S(2)}) copy-start(bf16[1,256,768]{2,1,0:T(8,128)(2,1)} %param.7) | copy-start | bytes 1179652
  114.5 28.0 %collective-permute-start.2 = (bf16[1,256,768]{2,1,0:T(8,128)(2,1)}, bf16[1,256,768]{2,1,0:T(8,128)(2,1)S(1)}, u32[]{:S(2)}, u32[]{:S(2)}) collective-permute-start(bf16[1,256,768]{2,1,0:T(8,128)(2,1)} %get-tuple-element.8), channel_id=1, source_target_pairs={{0,4},{2,6},{4,8},{6,10},{8,12},{10,14},{12,16},{14,18},{16,20},{1... | collective-permute-start | bytes 1179656 | tf_op jit(solution)/shard_map/ppermute | solution.py:26
  116.8 26.9 %collective-permute-start.3 = (bf16[1,256,768]{2,1,0:T(8,128)(2,1)}, bf16[1,256,768]{2,1,0:T(8,128)(2,1)S(1)}, u32[]{:S(2)}, u32[]{:S(2)}) collective-permute-start(bf16[1,256,768]{2,1,0:T(8,128)(2,1)} %get-tuple-element.8), channel_id=1, source_target_pairs={{4,0},{6,2},{8,4},{10,6},{12,8},{14,10},{16,12},{18,14},{20,16},{2... | collective-permute-start | bytes 1179656 | tf_op jit(solution)/shard_map/ppermute | solution.py:26
  135.8 14.7 %collective-permute-start.10 = (bf16[1,256,384]{2,1,0:T(8,128)(2,1)}, bf16[1,256,384]{2,1,0:T(8,128)(2,1)}, u32[]{:S(2)}, u32[]{:S(2)}) collective-permute-start(bf16[1,256,384]{2,1,0:T(8,128)(2,1)} %fusion.74), channel_id=1, source_target_pairs={{0,4},{2,6},{4,8},{6,10},{8,12},{10,14},{12,16},{14,18},{16,20},{1... | collective-permute-start | bytes 589832 | tf_op jit(solution)/shard_map/ppermute | solution.py:26
  139.9 12.1 %collective-permute-start.9 = (bf16[1,256,384]{2,1,0:T(8,128)(2,1)}, bf16[1,256,384]{2,1,0:T(8,128)(2,1)}, u32[]{:S(2)}, u32[]{:S(2)}) collective-permute-start(bf16[1,256,384]{2,1,0:T(8,128)(2,1)} %fusion.74), channel_id=1, source_target_pairs={{4,0},{6,2},{8,4},{10,6},{12,8},{14,10},{16,12},{18,14},{20,16},{2... | collective-permute-start | bytes 589832 | tf_op jit(solution)/shard_map/ppermute | solution.py:26
  147.7 16.9 %collective-permute-start.4 = (bf16[1,256,768]{2,1,0:T(8,128)(2,1)}, bf16[1,256,768]{2,1,0:T(8,128)(2,1)S(1)}, u32[]{:S(2)}, u32[]{:S(2)}) collective-permute-start(bf16[1,256,768]{2,1,0:T(8,128)(2,1)} %fusion.5), channel_id=1, source_target_pairs={{1,0},{0,1},{3,2},{2,3},{5,4},{4,5},{7,6},{6,7},{9,8},{8,9},{11,10... | collective-permute-start | bytes 1179656 | tf_op jit(solution)/shard_map/ppermute | solution.py:32
  150.5 3.5 %copy-start.5 = (bf16[1,2,384,768]{3,2,1,0:T(8,128)(2,1)S(1)}, bf16[1,2,384,768]{3,2,1,0:T(8,128)(2,1)}, u32[]{:S(2)}) copy-start(bf16[1,2,384,768]{3,2,1,0:T(8,128)(2,1)} %all-gather.5.cloned.1.call-done) | copy-start | bytes 3538948
  150.5 3.5 %copy-start.7 = (f32[1,256,384]{2,1,0:T(8,128)S(1)}, f32[1,256,384]{2,1,0:T(8,128)}, u32[]{:S(2)}) copy-start(f32[1,256,384]{2,1,0:T(8,128)} %fusion.12) | copy-start | bytes 1179652
  154.0 9.2 %copy-start.3 = (bf16[1,256,768]{2,1,0:T(8,128)(2,1)S(1)}, bf16[1,256,768]{2,1,0:T(8,128)(2,1)}, u32[]{:S(2)}) copy-start(bf16[1,256,768]{2,1,0:T(8,128)(2,1)} %param.6) | copy-start | bytes 1179652
  154.5 6.9 %collective-permute-start.12 = (bf16[1,128,384]{2,1,0:T(8,128)(2,1)S(1)}, bf16[1,128,384]{2,1,0:T(8,128)(2,1)S(1)}, u32[]{:S(2)}, u32[]{:S(2)}) collective-permute-start(bf16[1,128,384]{2,1,0:T(8,128)(2,1)S(1)} %get-tuple-element.7), channel_id=1, source_target_pairs={{0,2},{2,4},{4,6},{6,8},{8,10},{10,12},{12,14},{14,16},{16,18},{18... | collective-permute-start | bytes 294920 | tf_op jit(solution)/shard_map/ppermute | solution.py:17
  156.5 6.7 %collective-permute-start.11 = (bf16[1,128,384]{2,1,0:T(8,128)(2,1)S(1)}, bf16[1,128,384]{2,1,0:T(8,128)(2,1)S(1)}, u32[]{:S(2)}, u32[]{:S(2)}) collective-permute-start(bf16[1,128,384]{2,1,0:T(8,128)(2,1)S(1)} %get-tuple-element.6), channel_id=1, source_target_pairs={{2,0},{4,2},{6,4},{8,6},{10,8},{12,10},{14,12},{16,14},{18,16},{20... | collective-permute-start | bytes 294920 | tf_op jit(solution)/shard_map/ppermute | solution.py:18
  164.0 11.6 %collective-permute-start.13 = (bf16[1,256,768]{2,1,0:T(8,128)(2,1)S(1)}, bf16[1,256,768]{2,1,0:T(8,128)(2,1)S(1)}, u32[]{:S(2)}, u32[]{:S(2)}) collective-permute-start(bf16[1,256,768]{2,1,0:T(8,128)(2,1)S(1)} %fusion.28), channel_id=1, source_target_pairs={{1,0},{0,1},{3,2},{2,3},{5,4},{4,5},{7,6},{6,7},{9,8},{8,9},{11,10... | collective-permute-start | bytes 1179656 | tf_op jit(solution)/shard_map/ppermute | solution.py:32
Sparse Core Ops, SparseCore 0:
  10.3 49.3 all-gather.2
  61.9 35.7 all-gather.4
where the time goes:
time: 186 us; the launch traced here: 184 us
  waiting for transfers between devices  89.5 us (48%)
  starting transfers between devices  41.9 us (23%)
  matrix products  32.6 us (18%)
  between operations  14.4 us (8%)
  local copies, waits for them, and re-layouts  3.09 us (2%)
  other arithmetic  2.54 us (1%)
    all_gather x1, waiting for transfers between devices, local(): lax.all_gather(conv_weight, 'seq', axis=3, tiled=True)  34 us
    all_gather x1, waiting for transfers between devices, local(): lax.all_gather(proj_weight, 'seq', axis=2, tiled=True)  32.6 us
    ppermute x6, starting transfers between devices, from_behind(): return lax.ppermute(block, axis, route)  20.3 us
    dot_general x10, matrix products, conv_apply(): jnp.einsum('krc,ch->krh', values, weight, preferred_element_type=jnp.floa...  15.6 us
    ppermute x3, starting transfers between devices, padded(): after = lax.ppermute(initial, axis, down)  13.6 us
    ppermute x2, waiting for transfers between devices, from_behind_2(): return lax.ppermute(block, axis, route)  11 us
    ppermute x6, waiting for transfers between devices, from_behind(): return lax.ppermute(block, axis, route)  9.06 us
    dot_general x3, matrix products, run_forward(): jnp.einsum('krh,hc->krc', hidden, proj_part, preferred_element_type=jnp.f...  9.04 us
  transfers between devices with their start and end apart: 16, of which 6 were waited for; matrix products, arithmetic and copies ran while one was open for 20% of the time, Pallas kernels for 0%

commit v1 on v0

v1 whole, which is shorter than its diff:
```python
import functools

import jax
import jax.numpy as jnp
from jax import lax
from jax.experimental import pallas as pl
from jax.experimental.pallas import tpu as pltpu
from jax.sharding import PartitionSpec as P

BLOCKS = 2
FIRST_DILATION = 128
MESH = pl.DeviceIdType.MESH
F32 = jnp.float32
BF16 = jnp.bfloat16
K0 = 0.7978845608028654
K1 = 0.044715
UP, DOWN, ACROSS, SIB = range(4)
CHUNK = 64


def gelu(x):
    return x * (0.5 * (1.0 + jnp.tanh(K0 * (x + K1 * (x * x * x)))))


def gelu_slope(x):
    square = x * x
    t = jnp.tanh(K0 * (x + K1 * (square * x)))
    return 0.5 * (1.0 + t) + x * (0.5 * (1.0 - t * t)) * (K0 * (1.0 + 3.0 * K1 * square))


def dot(a, b):
    return jnp.dot(a, b, preferred_element_type=F32)


def dot_t(a, b):
    return lax.dot_general(a, b, (((1,), (1,)), ((), ())), preferred_element_type=F32)


def by_rows(total, body):
    @pl.loop(0, total // CHUNK)
    def _(j):
        body(pl.ds(pl.multiple_of(j * CHUNK, CHUNK), CHUNK))


def kernel(n, sections, gather, fx, bx, bg, cw, pw, o_next, o_prev, *scratch):
    (wc, pg, pf, act, state, send0, recv0, send1, recv1, pre, slope, dh, e_buf, recv_e1, recv_e0, part, grad,
     out_f, out_b, g_send, g_recv, h_send, h_recv) = scratch
    rows, half = fx.shape[1], FIRST_DILATION
    me, sec = lax.axis_index("seq"), lax.axis_index("section")
    depth = n // 4
    core, chip = lax.rem(me, 2), me // 2
    x, z = lax.rem(chip, 2), chip // 2
    n_z = depth

    def at(zz, xx, cc):
        return (zz * 2 + xx) * 2 + cc

    def to_seq(index):
        return {"seq": index}

    target = {UP: me + 4, DOWN: me - 4, ACROSS: at(z, 1 - x, core), SIB: at(z, x, 1 - core)}

    barrier = pltpu.get_barrier_semaphore()

    def greet(device):
        pl.semaphore_signal(barrier, inc=1, device_id=device, device_id_type=MESH)

    near = [(-1, me >= 1), (1, me < n - 1), (-2, me >= 2), (2, me < n - 2)]
    if gather:
        near += [(-4, z > 0), (4, z < n_z - 1)]
    count = jnp.int32(2)
    for gap, there in near:
        count = count + there.astype(jnp.int32)

        @pl.when(there)
        def _(gap=gap):
            greet(to_seq(me + gap))

    if gather:
        count = count + 2
        greet(to_seq(target[ACROSS]))
        greet(to_seq(target[SIB]))
    next_sec, prev_sec = lax.rem(sec + 1, sections), lax.rem(sec + sections - 1, sections)
    greet({"section": next_sec})
    greet({"section": prev_sec})

    for side, none0, none1 in ((0, me < 1, me < 2), (1, me >= n - 1, me >= n - 2)):
        @pl.when(none0)
        def _(side=side):
            for p in range(2):
                recv0[p, side] = jnp.zeros(recv0.shape[2:], BF16)
            recv_e0[side] = jnp.zeros(recv_e0.shape[1:], BF16)

        @pl.when(none1)
        def _(side=side):
            for p in range(2):
                recv1[p, side] = jnp.zeros(recv1.shape[2:], BF16)
            recv_e1[side] = jnp.zeros(recv_e1.shape[1:], BF16)

    if gather:
        c_rows = cw.shape[3]
        h_rows = pw.shape[2]

        def piece(t, owner):
            if t % 2 == 0:
                return wc.at[t // 2, :, pl.ds(pl.multiple_of(owner * c_rows, 16), c_rows), :]
            return pg.at[t // 2, owner]

        def copy(t, zz, xx, cc, kind):
            owner = at(zz, xx, cc)
            return pltpu.make_async_remote_copy(
                src_ref=piece(t, owner), dst_ref=piece(t, owner),
                send_sem=g_send.at[t, kind, zz * 2 + xx], recv_sem=g_recv.at[t, owner],
                device_id=to_seq(target[kind]), device_id_type=MESH)

        own = pl.ds(pl.multiple_of(me * c_rows, 16), c_rows)
        for b in range(BLOCKS):
            for k in range(3):
                wc[b, k, own, :] = cw[0, b, k]
            p32 = pw[0, b].astype(F32)
            width = p32.shape[1] // 2
            pg[b, me] = jnp.concatenate([p32[:, :width], p32[:, width:]], axis=0).astype(BF16)

        def step(t, k):
            if k == 0:
                @pl.when(z < n_z - 1)
                def _():
                    copy(t, z, x, core, UP).start()

                @pl.when(z > 0)
                def _():
                    copy(t, z, x, core, DOWN).start()
                copy(t, z, x, core, ACROSS).start()
                copy(t, z, x, core, SIB).start()
                return
            if k < n_z:
                @pl.when(z - k >= 0)
                def _():
                    copy(t, z - k, x, core, SIB).wait_recv()

                    @pl.when(z < n_z - 1)
                    def _():
                        copy(t, z - k, x, core, UP).start()
                    copy(t, z - k, x, core, ACROSS).start()
                    copy(t, z - k, x, core, SIB).start()

                @pl.when(z + k < n_z)
                def _():
                    copy(t, z + k, x, core, SIB).wait_recv()

                    @pl.when(z > 0)
                    def _():
                        copy(t, z + k, x, core, DOWN).start()
                    copy(t, z + k, x, core, ACROSS).start()
                    copy(t, z + k, x, core, SIB).start()
            far = k - 1
            if far == 0:
                copy(t, z, 1 - x, core, SIB).wait_recv()
                copy(t, z, 1 - x, core, SIB).start()
            else:
                for zz, there in ((z - far, z - far >= 0), (z + far, z + far < n_z)):
                    @pl.when(there)
                    def _(zz=zz):
                        copy(t, zz, 1 - x, core, SIB).wait_recv()
                        copy(t, zz, 1 - x, core, SIB).start()

        def settle(t):
            for zz in range(n_z):
                for xx in range(2):
                    copy(t, zz, xx, 1 - core, SIB).wait_recv()

        def drain(t):
            for zz in range(n_z):
                @pl.when((zz <= z) & (z < n_z - 1))
                def _(zz=zz):
                    copy(t, zz, x, core, UP).wait_send()

                @pl.when((zz >= z) & (z > 0))
                def _(zz=zz):
                    copy(t, zz, x, core, DOWN).wait_send()
                copy(t, zz, x, core, ACROSS).wait_send()
                for xx in range(2):
                    copy(t, zz, xx, core, SIB).wait_send()

        def join_proj(b):
            for j in range(n // 2):
                tall = []
                for owner in (2 * j, 2 * j + 1):
                    v = pg[b, owner].astype(F32)
                    tall.append(jnp.concatenate([v[:h_rows], v[h_rows:]], axis=1))
                pf[b, 2 * j * h_rows : 2 * (j + 1) * h_rows, :] = jnp.concatenate(tall, axis=0).astype(BF16)

        def conv_w(b, k):
            return wc[b, k]

        def proj_w(b):
            return pf[b]
    else:
        def step(t, k):
            pass

        settle = drain = join_proj = lambda t: None

        def conv_w(b, k):
            return cw[0, b, k]

        def proj_w(b):
            return pw[0, b]

    pl.semaphore_wait(barrier, count)
    step(0, 0)
    step(1, 0)

    def link(slot, src, dst, gap):
        return pltpu.make_async_remote_copy(
            src_ref=src, dst_ref=dst, send_sem=h_send.at[slot], recv_sem=h_recv.at[slot],
            device_id=to_seq(me + gap), device_id_type=MESH)

    def exchange(slot, sources, targets, gap, what):
        for side in range(2):
            ahead = (me < n - gap) if side == 0 else (me >= gap)
            behind = (me >= gap) if side == 0 else (me < n - gap)
            c = functools.partial(link, slot + side, sources[side], targets[side], gap if side == 0 else -gap)
            if what == "start":
                @pl.when(ahead)
                def _(c=c):
                    c().start()
            elif what == "send":
                @pl.when(ahead)
                def _(c=c):
                    c().wait_send()
            else:
                @pl.when(behind)
                def _(c=c):
                    c().wait_recv()

    def halo(b, p, what):
        if b == 0:
            exchange(2 * p, (send0.at[p, 0], send0.at[p, 1]), (recv0.at[p, 0], recv0.at[p, 1]), 1, what)
        else:
            exchange(4 + 2 * p, (send1.at[p, 0], send1.at[p, 1]), (recv1.at[p, 0], recv1.at[p, 1]), 2, what)

    def halo_e(b, what):
        if b == 1:
            exchange(8, (e_buf.at[1], e_buf.at[1]), (recv_e1.at[0], recv_e1.at[1]), 2, what)
        else:
            exchange(10, (e_buf.at[0, pl.ds(rows - half, half)], e_buf.at[0, pl.ds(0, half)]),
                     (recv_e0.at[0], recv_e0.at[1]), 1, what)

    inputs = (fx, bx)

    def activate(p, src):
        def body(r):
            act[p, r, :] = gelu(src[r, :].astype(F32)).astype(BF16)
        by_rows(rows, body)

    def taps(b, p):
        a = act[p]
        q0 = dot(a, conv_w(b, 0)).astype(BF16)
        q2 = dot(a, conv_w(b, 2)).astype(BF16)
        if b == 0:
            send0[p, 0] = q0[rows - half :]
            send0[p, 1] = q2[:half]
            halo(b, p, "start")
            pre[p, :half, :] = q2[half:].astype(F32)
            pre[p, half:, :] = q0[: rows - half].astype(F32)
            pre[p] = pre[p] + dot(a, conv_w(b, 1))
        else:
            send1[p, 0] = q0
            send1[p, 1] = q2
            halo(b, p, "start")
            pre[p] = dot(a, conv_w(b, 1))

    def finish(b, p, r):
        if b == 0:
            raise NotImplementedError
        return pre[p, r, :] + recv1[p, 0, r, :].astype(F32) + recv1[p, 1, r, :].astype(F32)

    def hidden0(p):
        halo(0, p, "recv")
        for side in range(2):
            def body(j, side=side):
                r = pl.ds(side * half + j * CHUNK, CHUNK)
                y = pre[p, r, :] + recv0[p, side, pl.ds(j * CHUNK, CHUNK), :].astype(F32)
                dh[p, r, :] = gelu(y).astype(BF16)
                if p == 1:
                    slope[0, r, :] = gelu_slope(y)
            for j in range(half // CHUNK):
                body(j)

    def advance(p):
        part[...] = dot(dh[p], proj_w(0))
        src = inputs[p]

        def body(r):
            h = (src[0, r, :].astype(F32) + part[r, :]).astype(BF16)
            state[p, r, :] = h
            act[p, r, :] = gelu(h.astype(F32)).astype(BF16)
        by_rows(rows, body)

    activate(1, bx.at[0])
    activate(0, fx.at[0])
    step(0, 1)
    step(1, 1)
    step(2, 0)
    for k in range(2, n_z + 1):
        step(0, k)
        step(1, k)
        if k < n_z:
            step(2, k - 1)
    step(3, 0)
    settle(0)
    taps(0, 1)
    taps(0, 0)
    step(2, n_z - 1)
    step(3, 1)
    settle(1)
    join_proj(0)
    hidden0(1)
    advance(1)
    step(2, n_z)
    step(3, 2)
    hidden0(0)
    advance(0)
    for k in range(3, n_z + 1):
        step(3, k)

    settle(2)
    taps(1, 1)
    taps(1, 0)
    settle(3)
    join_proj(1)
    part_h = part.at[:, pl.ds(0, pre.shape[2])]
    part_h[...] = dot_t(bg[0], proj_w(1))
    halo(1, 1, "recv")

    def body(r):
        e_buf[1, r, :] = (gelu_slope(finish(1, 1, r)) * part[r, : pre.shape[2]]).astype(BF16)
    by_rows(rows, body)
    halo_e(1, "start")

    halo(1, 0, "recv")

    def body(r):
        dh[0, r, :] = gelu(finish(1, 0, r)).astype(BF16)
    by_rows(rows, body)
    part[...] = dot(dh[0], proj_w(1))

    def body(r):
        out_f[r, :] = (state[0, r, :].astype(F32) + part[r, :]).astype(BF16)
    by_rows(rows, body)
    forward = pltpu.make_async_remote_copy(
        src_ref=out_f, dst_ref=o_next.at[0], send_sem=h_send.at[12], recv_sem=h_recv.at[12],
        device_id={"section": next_sec}, device_id_type=MESH)
    forward.start()

    part[...] = dot_t(e_buf[1], conv_w(1, 1))
    halo_e(1, "recv")
    part[...] = part[...] + dot_t(recv_e1[1], conv_w(1, 0)) + dot_t(recv_e1[0], conv_w(1, 2))

    def body(r):
        g = bg[0, r, :].astype(F32) + gelu_slope(state[1, r, :].astype(F32)) * part[r, :]
        grad[r, :] = g.astype(BF16)
    by_rows(rows, body)

    d0 = dot_t(grad[...], proj_w(0))
    e_buf[0] = (slope[0] * d0).astype(BF16)
    halo_e(0, "start")
    e = e_buf[0]
    part[...] = dot_t(e, conv_w(0, 1))
    part[: rows - half, :] = part[: rows - half, :] + dot_t(e_buf[0, half:, :], conv_w(0, 0))
    part[half:, :] = part[half:, :] + dot_t(e_buf[0, : rows - half, :], conv_w(0, 2))
    halo_e(0, "recv")
    part[rows - half :, :] = part[rows - half :, :] + dot_t(recv_e0[1], conv_w(0, 0))
    part[:half, :] = part[:half, :] + dot_t(recv_e0[0], conv_w(0, 2))

    def body(r):
        g = grad[r, :].astype(F32) + gelu_slope(bx[0, r, :].astype(F32)) * part[r, :]
        out_b[r, :] = g.astype(BF16)
    by_rows(rows, body)
    backward = pltpu.make_async_remote_copy(
        src_ref=out_b, dst_ref=o_prev.at[0], send_sem=h_send.at[13], recv_sem=h_recv.at[13],
        device_id={"section": prev_sec}, device_id_type=MESH)
    backward.start()

    for t in range(4):
        drain(t)
    for b in range(2):
        for p in range(2):
            halo(b, p, "send")
        halo_e(b, "send")
    forward.wait()
    backward.wait()


def local(n, sections, fwd_input, bwd_input, bwd_cotangent, conv_weight, proj_weight):
    rows, wide = fwd_input.shape[1:]
    narrow = conv_weight.shape[-1]
    half = FIRST_DILATION
    c_rows, h_rows = conv_weight.shape[3], proj_weight.shape[2]
    gather = c_rows % 16 == 0 and h_rows % 8 == 0
    if not gather:
        conv_weight = lax.all_gather(conv_weight, "seq", axis=3, tiled=True)
        proj_weight = lax.all_gather(proj_weight, "seq", axis=2, tiled=True)
    vm = pltpu.VMEM
    if gather:
        big = [
            vm((BLOCKS, 3, wide, narrow), BF16),
            vm((BLOCKS, n, 2 * h_rows, wide // 2), BF16),
            vm((BLOCKS, narrow, wide), BF16),
        ]
        g_sems = [pltpu.SemaphoreType.DMA((4, 4, n // 2)), pltpu.SemaphoreType.DMA((4, n))]
    else:
        big = [vm((16, 128), BF16)] * 3
        g_sems = [pltpu.SemaphoreType.DMA((1,)), pltpu.SemaphoreType.DMA((1,))]
    scratch = big + [
        vm((2, rows, wide), BF16),
        vm((2, rows, wide), BF16),
        vm((2, 2, half, narrow), BF16),
        vm((2, 2, half, narrow), BF16),
        vm((2, 2, rows, narrow), BF16),
        vm((2, 2, rows, narrow), BF16),
        vm((2, rows, narrow), F32),
        vm((1, rows, narrow), F32),
        vm((2, rows, narrow), BF16),
        vm((2, rows, narrow), BF16),
        vm((2, rows, narrow), BF16),
        vm((2, half, narrow), BF16),
        vm((rows, wide), F32),
        vm((rows, wide), BF16),
        vm((rows, wide), BF16),
        vm((rows, wide), BF16),
        *g_sems,
        pltpu.SemaphoreType.DMA((14,)),
        pltpu.SemaphoreType.DMA((14,)),
    ]
    shape = jax.ShapeDtypeStruct(fwd_input.shape, BF16)
    flops = 24 * 2 * rows * wide * narrow
    return pl.pallas_call(
        functools.partial(kernel, n, sections, gather),
        out_shape=(shape, shape),
        in_specs=[pl.BlockSpec(memory_space=pltpu.VMEM)] * 5,
        out_specs=(pl.BlockSpec(memory_space=pl.ANY),) * 2,
        scratch_shapes=scratch,
        cost_estimate=pl.CostEstimate(flops=flops, bytes_accessed=8 * rows * wide, transcendentals=9 * rows * wide),
        compiler_params=pltpu.CompilerParams(
            collective_id=0, has_side_effects=True, vmem_limit_bytes=48 * 1024 * 1024),
    )(fwd_input, bwd_input, bwd_cotangent, conv_weight, proj_weight)


def solution(mesh):
    in_specs = (
        P("section", "seq", None),
        P("section", "seq", None),
        P("section", "seq", None),
        P("section", None, None, "seq", None),
        P("section", None, "seq", None),
    )
    out_specs = (P("section", "seq", None), P("section", "seq", None))
    body = functools.partial(local, mesh.shape["seq"], mesh.shape["section"])
    return jax.shard_map(body, mesh=mesh, in_specs=in_specs, out_specs=out_specs, check_vma=False)
```

time: 186 us -> 90.3 us (0.49)
  waiting for transfers between devices: 89.5 us -> 0 us
  Pallas kernels: 0 us -> 83.1 us
  starting transfers between devices: 41.9 us -> 0 us
  matrix products: 32.6 us -> 0 us
  between operations: 14.4 us -> 0.65 us
  local copies, waits for them, and re-layouts: 3.09 us -> 6.29 us
  other arithmetic: 2.54 us -> 0 us
    pallas_call x0 -> x1, Pallas kernels: none -> 83.1 us  [local(): pl.pallas_call(functools.partial(kernel, n, sections, gather), out_shape=...]
    all_gather x2 -> x0, waiting for transfers between devices: 66.6 us -> none  [the longest x1 34 us: local(): lax.all_gather(conv_weight, 'seq', axis=3, tiled=True)]
    ppermute x14 -> x0, starting transfers between devices: 41.8 us -> none  [the longest x6 20.3 us: from_behind(): return lax.ppermute(block, axis, route)]
    dot_general x21 -> x0, matrix products: 32.6 us -> none  [the longest x10 15.6 us: conv_apply(): jnp.einsum('krc,ch->krh', values, weight, preferred_element_type=jnp.floa...]
    ppermute x14 -> x0, waiting for transfers between devices: 21.5 us -> none  [the longest x2 11 us: from_behind_2(): return lax.ppermute(block, axis, route)]
    unnamed x18 -> x12, local copies, waits for them, and re-layouts: 2.26 us -> 6.29 us
    convert_element_type x2 -> x0, other arithmetic: 2.54 us -> none  [run_forward(): jax.nn.gelu(present_state.astype(jnp.float32)).astype(jnp.bfloat16)]
  transfers between devices with their start and end apart: 16 -> 0, of which waited for: 6 -> 0; matrix products, arithmetic and copies ran while one was open for 20% -> 0% of each run, Pallas kernels for 0% -> 0%
where the time goes in v1:
time: 90.3 us; the launch traced here: 90 us
  Pallas kernels  83.1 us (92%)
  local copies, waits for them, and re-layouts  6.29 us (7%)
    pallas_call x1, Pallas kernels, local(): pl.pallas_call(functools.partial(kernel, n, sections, gather), out_shape=...  83.1 us
    unnamed x12, local copies, waits for them, and re-layouts  6.29 us

profile of v1, /device:TPU:8, one launch (start us, length us, event | category | flops | bytes accessed | tf_op | source)
XLA Modules:
  0.0 90.0 jit_solution(6560635038350847075)
XLA Ops:
  0.6 0.0 copy-start
  0.6 1.0 %copy-done = bf16[1,256,768]{2,1,0:T(8,128)(2,1)S(1)} copy-done((bf16[1,256,768]{2,1,0:T(8,128)(2,1)S(1)}, bf16[1,256,768]{2,1,0:T(8,128)(2,1)}, u32[]{:S(2)}) %copy-start) | copy-done | bytes 393240
  1.6 0.0 copy-start.1
  1.6 1.0 %copy-done.1 = bf16[1,256,768]{2,1,0:T(8,128)(2,1)S(1)} copy-done((bf16[1,256,768]{2,1,0:T(8,128)(2,1)S(1)}, bf16[1,256,768]{2,1,0:T(8,128)(2,1)}, u32[]{:S(2)}) %copy-start.1) | copy-done | bytes 393240
  2.6 0.0 copy-start.2
  2.6 1.0 %copy-done.2 = bf16[1,256,768]{2,1,0:T(8,128)(2,1)S(1)} copy-done((bf16[1,256,768]{2,1,0:T(8,128)(2,1)S(1)}, bf16[1,256,768]{2,1,0:T(8,128)(2,1)}, u32[]{:S(2)}) %copy-start.2) | copy-done | bytes 393240
  3.6 0.0 copy-start.3
  3.6 0.9 %copy-done.3 = bf16[1,2,3,48,384]{4,3,2,1,0:T(8,128)(2,1)S(1)} copy-done((bf16[1,2,3,48,384]{4,3,2,1,0:T(8,128)(2,1)S(1)}, bf16[1,2,3,48,384]{4,3,2,1,0:T(8,128)(2,1)}, u32[]{:S(2)}) %copy-start.3) | copy-done | bytes 221208
  4.6 0.0 copy-start.4
  4.6 0.9 copy-done.4
  5.4 83.1 %shard_map.68 = (bf16[1,256,768]{2,1,0:T(8,128)(2,1)S(1)}, bf16[1,256,768]{2,1,0:T(8,128)(2,1)S(1)}) custom-call(bf16[1,256,768]{2,1,0:T(8,128)(2,1)S(1)} %copy-done, bf16[1,256,768]{2,1,0:T(8,128)(2,1)S(1)} %copy-done.1, bf16[1,256,768]{2,1,0:T(8,128)(2,1)S(1)} %copy-done.2, bf16[1,2,3,48,384]{4,3,2,1,0:T(8,128)(2,1)S(1)} %copy-done.3, ...), custom_call_target="tpu_custom_call" | custom-call | flops 3623878656 | bytes 1572864 | tf_op jit(solution)/shard_map/pallas_call | solution.py:439
  88.5 0.7 copy.9
  89.3 0.7 copy.10
Async XLA Ops:
  0.6 1.0 %copy-start = (bf16[1,256,768]{2,1,0:T(8,128)(2,1)S(1)}, bf16[1,256,768]{2,1,0:T(8,128)(2,1)}, u32[]{:S(2)}) copy-start(bf16[1,256,768]{2,1,0:T(8,128)(2,1)} %fx.1) | copy-start | bytes 1179652
  1.6 1.0 %copy-start.1 = (bf16[1,256,768]{2,1,0:T(8,128)(2,1)S(1)}, bf16[1,256,768]{2,1,0:T(8,128)(2,1)}, u32[]{:S(2)}) copy-start(bf16[1,256,768]{2,1,0:T(8,128)(2,1)} %bx.1) | copy-start | bytes 1179652
  2.6 1.0 %copy-start.2 = (bf16[1,256,768]{2,1,0:T(8,128)(2,1)S(1)}, bf16[1,256,768]{2,1,0:T(8,128)(2,1)}, u32[]{:S(2)}) copy-start(bf16[1,256,768]{2,1,0:T(8,128)(2,1)} %bg.1) | copy-start | bytes 1179652
  3.6 0.9 %copy-start.3 = (bf16[1,2,3,48,384]{4,3,2,1,0:T(8,128)(2,1)S(1)}, bf16[1,2,3,48,384]{4,3,2,1,0:T(8,128)(2,1)}, u32[]{:S(2)}) copy-start(bf16[1,2,3,48,384]{4,3,2,1,0:T(8,128)(2,1)} %cw.1) | copy-start | bytes 663556
  4.6 0.9 copy-start.4

commit v2 on v1

--- a/solution.py
+++ b/solution.py
@@ -16,6 +16,9 @@
 K1 = 0.044715
 UP, DOWN, ACROSS, SIB = range(4)
 CHUNK = 64
+SLOT = (0, 2, 1)
+PIECES = 5
+LIGHT = (3, 4)
 
 
 def gelu(x):
@@ -42,9 +45,9 @@
         body(pl.ds(pl.multiple_of(j * CHUNK, CHUNK), CHUNK))
 
 
-def kernel(n, sections, gather, fx, bx, bg, cw, pw, o_next, o_prev, *scratch):
+def kernel(n, sections, gather, fx_hbm, bx_hbm, bg_hbm, cw_hbm, pw_hbm, o_next, o_prev, *scratch):
     (wc, pg, pf, act, state, send0, recv0, send1, recv1, pre, slope, dh, e_buf, recv_e1, recv_e0, part, grad,
-     out_f, out_b, g_send, g_recv, h_send, h_recv) = scratch
+     out_f, out_b, fx, bx, bg, pw, g_send, g_recv, h_send, h_recv, l_sem) = scratch
     rows, half = fx.shape[1], FIRST_DILATION
     me, sec = lax.axis_index("seq"), lax.axis_index("section")
     depth = n // 4
@@ -59,6 +62,23 @@
         return {"seq": index}
 
     target = {UP: me + 4, DOWN: me - 4, ACROSS: at(z, 1 - x, core), SIB: at(z, x, 1 - core)}
+
+    loads = []
+
+    def load(src, dst):
+        c = pltpu.make_async_copy(src, dst, l_sem.at[len(loads)])
+        c.start()
+        loads.append(c)
+
+    wide_rows = cw_hbm.shape[3]
+    own = pl.ds(pl.multiple_of(me * wide_rows, 16), wide_rows) if gather else pl.ds(0, wide_rows)
+    load(pw_hbm, pw)
+    for b in range(BLOCKS):
+        for k in range(3):
+            load(cw_hbm.at[0, b, k], wc.at[b, SLOT[k], own, :])
+    weight_loads = len(loads)
+    for src, dst in ((bx_hbm, bx), (fx_hbm, fx), (bg_hbm, bg)):
+        load(src, dst)
 
     barrier = pltpu.get_barrier_semaphore()
 
@@ -98,13 +118,15 @@
             recv_e1[side] = jnp.zeros(recv_e1.shape[1:], BF16)
 
     if gather:
-        c_rows = cw.shape[3]
+        c_rows = wide_rows
         h_rows = pw.shape[2]
 
         def piece(t, owner):
-            if t % 2 == 0:
-                return wc.at[t // 2, :, pl.ds(pl.multiple_of(owner * c_rows, 16), c_rows), :]
-            return pg.at[t // 2, owner]
+            if t in (1, 4):
+                return pg.at[t // 3, owner]
+            block, low, taps_held = {0: (0, 0, 3), 2: (1, 0, 2), 3: (1, 2, 1)}[t]
+            span = pl.ds(pl.multiple_of(owner * c_rows, 16), c_rows)
+            return wc.at[block, pl.ds(low, taps_held), span, :]
 
         def copy(t, zz, xx, cc, kind):
             owner = at(zz, xx, cc)
@@ -113,10 +135,9 @@
                 send_sem=g_send.at[t, kind, zz * 2 + xx], recv_sem=g_recv.at[t, owner],
                 device_id=to_seq(target[kind]), device_id_type=MESH)
 
-        own = pl.ds(pl.multiple_of(me * c_rows, 16), c_rows)
+        for c in loads[:weight_loads]:
+            c.wait()
         for b in range(BLOCKS):
-            for k in range(3):
-                wc[b, k, own, :] = cw[0, b, k]
             p32 = pw[0, b].astype(F32)
             width = p32.shape[1] // 2
             pg[b, me] = jnp.concatenate([p32[:, :width], p32[:, width:]], axis=0).astype(BF16)
@@ -132,6 +153,31 @@
                     copy(t, z, x, core, DOWN).start()
                 copy(t, z, x, core, ACROSS).start()
                 copy(t, z, x, core, SIB).start()
+                return
+            if t in LIGHT:
+                def onward(zz, xx, kind):
+                    copy(t, zz, xx, core, SIB).wait_recv()
+                    if kind != DOWN:
+                        @pl.when(z < n_z - 1)
+                        def _():
+                            copy(t, zz, xx, core, UP).start()
+                    if kind != UP:
+                        @pl.when(z > 0)
+                        def _():
+                            copy(t, zz, xx, core, DOWN).start()
+                    copy(t, zz, xx, core, SIB).start()
+
+                if k == 1:
+                    onward(z, 1 - x, None)
+                for far, xx in ((k, x), (k - 1, 1 - x)):
+                    if 0 < far < n_z:
+                        @pl.when(z - far >= 0)
+                        def _(far=far, xx=xx):
+                            onward(z - far, xx, UP)
+
+                        @pl.when(z + far < n_z)
+                        def _(far=far, xx=xx):
+                            onward(z + far, xx, DOWN)
                 return
             if k < n_z:
                 @pl.when(z - k >= 0)
@@ -170,17 +216,23 @@
                     copy(t, zz, xx, 1 - core, SIB).wait_recv()
 
         def drain(t):
+            light = t in LIGHT
+            columns = (x, 1 - x) if light else (x,)
             for zz in range(n_z):
-                @pl.when((zz <= z) & (z < n_z - 1))
-                def _(zz=zz):
-                    copy(t, zz, x, core, UP).wait_send()
-
-                @pl.when((zz >= z) & (z > 0))
-                def _(zz=zz):
-                    copy(t, zz, x, core, DOWN).wait_send()
-                copy(t, zz, x, core, ACROSS).wait_send()
+                for xx in columns:
+                    @pl.when((zz <= z) & (z < n_z - 1))
+                    def _(zz=zz, xx=xx):
+                        copy(t, zz, xx, core, UP).wait_send()
+
+                    @pl.when((zz >= z) & (z > 0))
+                    def _(zz=zz, xx=xx):
+                        copy(t, zz, xx, core, DOWN).wait_send()
+                if not light:
+                    copy(t, zz, x, core, ACROSS).wait_send()
                 for xx in range(2):
                     copy(t, zz, xx, core, SIB).wait_send()
+            if light:
+                copy(t, z, x, core, ACROSS).wait_send()
 
         def join_proj(b):
             for j in range(n // 2):
@@ -190,26 +242,28 @@
                     tall.append(jnp.concatenate([v[:h_rows], v[h_rows:]], axis=1))
                 pf[b, 2 * j * h_rows : 2 * (j + 1) * h_rows, :] = jnp.concatenate(tall, axis=0).astype(BF16)
 
-        def conv_w(b, k):
-            return wc[b, k]
-
         def proj_w(b):
             return pf[b]
     else:
+        for c in loads[:weight_loads]:
+            c.wait()
+
         def step(t, k):
             pass
 
         settle = drain = join_proj = lambda t: None
 
-        def conv_w(b, k):
-            return cw[0, b, k]
-
         def proj_w(b):
             return pw[0, b]
 
+    def conv_w(b, k):
+        return wc[b, SLOT[k]]
+
     pl.semaphore_wait(barrier, count)
-    step(0, 0)
-    step(1, 0)
+    for t in range(3):
+        step(t, 0)
+    for c in loads[weight_loads:]:
+        c.wait()
 
     def link(slot, src, dst, gap):
         return pltpu.make_async_remote_copy(
@@ -258,22 +312,19 @@
         a = act[p]
         q0 = dot(a, conv_w(b, 0)).astype(BF16)
         q2 = dot(a, conv_w(b, 2)).astype(BF16)
-        if b == 0:
-            send0[p, 0] = q0[rows - half :]
-            send0[p, 1] = q2[:half]
-            halo(b, p, "start")
-            pre[p, :half, :] = q2[half:].astype(F32)
-            pre[p, half:, :] = q0[: rows - half].astype(F32)
-            pre[p] = pre[p] + dot(a, conv_w(b, 1))
-        else:
-            send1[p, 0] = q0
-            send1[p, 1] = q2
-            halo(b, p, "start")
-            pre[p] = dot(a, conv_w(b, 1))
+        send0[p, 0] = q0[rows - half :]
+        send0[p, 1] = q2[:half]
+        halo(b, p, "start")
+        pre[p, :half, :] = q2[half:].astype(F32)
+        pre[p, half:, :] = q0[: rows - half].astype(F32)
+        pre[p] = pre[p] + dot(a, conv_w(b, 1))
+
+    def outer(p):
+        send1[p, 0] = dot(act[p], conv_w(1, 0)).astype(BF16)
+        send1[p, 1] = dot(act[p], conv_w(1, 2)).astype(BF16)
+        halo(1, p, "start")
 
     def finish(b, p, r):
-        if b == 0:
-            raise NotImplementedError
         return pre[p, r, :] + recv1[p, 0, r, :].astype(F32) + recv1[p, 1, r, :].astype(F32)
 
     def hidden0(p):
@@ -300,35 +351,35 @@
 
     activate(1, bx.at[0])
     activate(0, fx.at[0])
-    step(0, 1)
-    step(1, 1)
-    step(2, 0)
-    for k in range(2, n_z + 1):
+    for k in range(1, n_z + 1):
         step(0, k)
         step(1, k)
-        if k < n_z:
-            step(2, k - 1)
-    step(3, 0)
+        if k == 1:
+            step(3, 0)
+            step(4, 0)
+        else:
+            for t in range(2, PIECES):
+                step(t, k - 1)
     settle(0)
     taps(0, 1)
+    step(2, n_z)
     taps(0, 0)
-    step(2, n_z - 1)
-    step(3, 1)
+    step(3, n_z)
+    step(4, n_z)
     settle(1)
     join_proj(0)
     hidden0(1)
     advance(1)
-    step(2, n_z)
-    step(3, 2)
     hidden0(0)
     advance(0)
-    for k in range(3, n_z + 1):
-        step(3, k)
 
     settle(2)
-    taps(1, 1)
-    taps(1, 0)
+    outer(1)
+    outer(0)
     settle(3)
+    pre[1] = dot(act[1], conv_w(1, 1))
+    pre[0] = dot(act[0], conv_w(1, 1))
+    settle(4)
     join_proj(1)
     part_h = part.at[:, pl.ds(0, pre.shape[2])]
     part_h[...] = dot_t(bg[0], proj_w(1))
@@ -346,13 +397,18 @@
     by_rows(rows, body)
     part[...] = dot(dh[0], proj_w(1))
 
-    def body(r):
+    chunks = rows // CHUNK
+
+    def ship(j, held, out, slot, section):
+        r = pl.ds(j * CHUNK, CHUNK)
+        return pltpu.make_async_remote_copy(
+            src_ref=held.at[r, :], dst_ref=out.at[0, r, :], send_sem=h_send.at[slot + j], recv_sem=h_recv.at[slot + j],
+            device_id={"section": section}, device_id_type=MESH)
+
+    for j in range(chunks):
+        r = pl.ds(j * CHUNK, CHUNK)
         out_f[r, :] = (state[0, r, :].astype(F32) + part[r, :]).astype(BF16)
-    by_rows(rows, body)
-    forward = pltpu.make_async_remote_copy(
-        src_ref=out_f, dst_ref=o_next.at[0], send_sem=h_send.at[12], recv_sem=h_recv.at[12],
-        device_id={"section": next_sec}, device_id_type=MESH)
-    forward.start()
+        ship(j, out_f, o_next, 12, next_sec).start()
 
     part[...] = dot_t(e_buf[1], conv_w(1, 1))
     halo_e(1, "recv")
@@ -374,23 +430,21 @@
     part[rows - half :, :] = part[rows - half :, :] + dot_t(recv_e0[1], conv_w(0, 0))
     part[:half, :] = part[:half, :] + dot_t(recv_e0[0], conv_w(0, 2))
 
-    def body(r):
+    for j in range(chunks):
+        r = pl.ds(j * CHUNK, CHUNK)
         g = grad[r, :].astype(F32) + gelu_slope(bx[0, r, :].astype(F32)) * part[r, :]
         out_b[r, :] = g.astype(BF16)
-    by_rows(rows, body)
-    backward = pltpu.make_async_remote_copy(
-        src_ref=out_b, dst_ref=o_prev.at[0], send_sem=h_send.at[13], recv_sem=h_recv.at[13],
-        device_id={"section": prev_sec}, device_id_type=MESH)
-    backward.start()
-
-    for t in range(4):
+        ship(j, out_b, o_prev, 12 + chunks, prev_sec).start()
+
+    for t in range(PIECES):
         drain(t)
     for b in range(2):
         for p in range(2):
             halo(b, p, "send")
         halo_e(b, "send")
-    forward.wait()
-    backward.wait()
+    for j in range(chunks):
+        ship(j, out_f, o_next, 12, next_sec).wait()
+        ship(j, out_b, o_prev, 12 + chunks, prev_sec).wait()
 
 
 def local(n, sections, fwd_input, bwd_input, bwd_cotangent, conv_weight, proj_weight):
@@ -409,9 +463,9 @@
             vm((BLOCKS, n, 2 * h_rows, wide // 2), BF16),
             vm((BLOCKS, narrow, wide), BF16),
         ]
-        g_sems = [pltpu.SemaphoreType.DMA((4, 4, n // 2)), pltpu.SemaphoreType.DMA((4, n))]
+        g_sems = [pltpu.SemaphoreType.DMA((PIECES, 4, n // 2)), pltpu.SemaphoreType.DMA((PIECES, n))]
     else:
-        big = [vm((16, 128), BF16)] * 3
+        big = [vm((BLOCKS, 3, wide, narrow), BF16), vm((16, 128), BF16), vm((16, 128), BF16)]
         g_sems = [pltpu.SemaphoreType.DMA((1,)), pltpu.SemaphoreType.DMA((1,))]
     scratch = big + [
         vm((2, rows, wide), BF16),
@@ -430,21 +484,24 @@
         vm((rows, wide), BF16),
         vm((rows, wide), BF16),
         vm((rows, wide), BF16),
+        *[vm((1, rows, wide), BF16)] * 3,
+        vm(proj_weight.shape, BF16),
         *g_sems,
-        pltpu.SemaphoreType.DMA((14,)),
-        pltpu.SemaphoreType.DMA((14,)),
+        pltpu.SemaphoreType.DMA((12 + 2 * (rows // CHUNK),)),
+        pltpu.SemaphoreType.DMA((12 + 2 * (rows // CHUNK),)),
+        pltpu.SemaphoreType.DMA((10,)),
     ]
     shape = jax.ShapeDtypeStruct(fwd_input.shape, BF16)
     flops = 24 * 2 * rows * wide * narrow
     return pl.pallas_call(
         functools.partial(kernel, n, sections, gather),
         out_shape=(shape, shape),
-        in_specs=[pl.BlockSpec(memory_space=pltpu.VMEM)] * 5,
+        in_specs=[pl.BlockSpec(memory_space=pltpu.HBM)] * 5,
         out_specs=(pl.BlockSpec(memory_space=pl.ANY),) * 2,
         scratch_shapes=scratch,
         cost_estimate=pl.CostEstimate(flops=flops, bytes_accessed=8 * rows * wide, transcendentals=9 * rows * wide),
         compiler_params=pltpu.CompilerParams(
-            collective_id=0, has_side_effects=True, vmem_limit_bytes=48 * 1024 * 1024),
+            collective_id=0, has_side_effects=True, vmem_limit_bytes=62 * 1024 * 1024),
     )(fwd_input, bwd_input, bwd_cotangent, conv_weight, proj_weight)
 
 

time: 90.3 us -> 83.7 us (0.927)
  local copies, waits for them, and re-layouts: 6.29 us -> 2.57 us
  Pallas kernels: 83.1 us -> 80.3 us
    unnamed x12 -> x4, local copies, waits for them, and re-layouts: 6.29 us -> 2.57 us
    pallas_call x1, Pallas kernels: 83.1 us -> 80.3 us  [local(): pl.pallas_call(functools.partial(kernel, n, sections, gather), out_shape=...]
where the time goes in v2:
time: 83.7 us; the launch traced here: 83.5 us
  Pallas kernels  80.3 us (96%)
  local copies, waits for them, and re-layouts  2.57 us (3%)
    pallas_call x1, Pallas kernels, local(): pl.pallas_call(functools.partial(kernel, n, sections, gather), out_shape=...  80.3 us
    unnamed x4, local copies, waits for them, and re-layouts  2.57 us

profile of v2, /device:TPU:8, one launch (start us, length us, event | category | flops | bytes accessed | tf_op | source)
XLA Modules:
  0.0 83.5 jit_solution(11555073957335706698)
XLA Ops:
  0.6 80.3 %shard_map.68 = (bf16[1,256,768]{2,1,0:T(8,128)(2,1)}, bf16[1,256,768]{2,1,0:T(8,128)(2,1)}) custom-call(bf16[1,256,768]{2,1,0:T(8,128)(2,1)} %fx_hbm.1, bf16[1,256,768]{2,1,0:T(8,128)(2,1)} %bx_hbm.1, bf16[1,256,768]{2,1,0:T(8,128)(2,1)} %bg_hbm.1, bf16[1,2,3,48,384]{4,3,2,1,0:T(8,128)(2,1)} %cw_hbm.1, bf16[1,2,24,768]{3,2,1,0:T(8,128)(2,1)} %pw_hbm.1), custom_call_target="tpu_custom_call" | custom-call | flops 3623878656 | bytes 1572864 | tf_op jit(solution)/shard_map/pallas_call | solution.py:496
  80.9 0.0 copy-start
  80.9 1.8 %copy.9 = bf16[1,256,768]{2,1,0:T(8,128)(2,1)} copy(bf16[1,256,768]{2,1,0:T(8,128)(2,1)} %get-tuple-element.4) | data formatting | bytes 786432
  82.8 0.0 copy-done
  82.8 0.7 copy.10
Async XLA Ops:
  80.9 1.8 %copy-start = (bf16[1,256,768]{2,1,0:T(8,128)(2,1)S(1)}, bf16[1,256,768]{2,1,0:T(8,128)(2,1)}, u32[]{:S(2)}) copy-start(bf16[1,256,768]{2,1,0:T(8,128)(2,1)} %get-tuple-element.5) | copy-start | bytes 1179652
